TPU v7x, 256 devices: a whole 4x4x8 slice. The times are simulated.
256 devices in a mesh: grp: 4 (over x_hi, core), ctx: 64 (over x_lo, z, y).
Axes of the slice: x: 4 (x_hi: 2, x_lo: 2; x = x_hi * 2 + x_lo), y: 4, z: 8, core: 2. Of those that a mesh axis runs over, the one named last changes fastest.
Arguments:
- queries: bfloat16 [65536, 28, 128], P(('grp', 'ctx')), may hold values from -12 to 12
- key_rows: bfloat16 [65536, 4, 128], P(('grp', 'ctx')), may hold values from -6 to 6
- value_rows: bfloat16 [65536, 4, 128], P(('grp', 'ctx')), may hold values from -6 to 6
- out_grad: bfloat16 [65536, 28, 128], P(('grp', 'ctx')), may hold values from -6 to 6
- doc_ids: int32 [65536], P(('grp', 'ctx')), may hold values from 0 to 127, never falling along the last dimension, each value on 1 to 768 neighbouring positions
Outputs:
- query_grad: bfloat16 [65536, 28, 128], P(('grp', 'ctx'))
- key_grad: bfloat16 [65536, 4, 128], P(('grp', 'ctx'))
- value_grad: bfloat16 [65536, 4, 128], P(('grp', 'ctx'))
Inputs may be any that keep to these rules, and one draw needn't show every extreme that they name: `doc_ids`: document numbers never fall along the tokens; every document has 1 to 768 tokens, and one has exactly 768.
All inputs are finite; a program needn't handle non-finite values.
Results may differ from a plain program's by a relative error of at most 0.0074.
Values may be sent and summed in bfloat16 or wider, within the bound.
A program may use at most 192 MiB of HBM per device.

v0:
```python
import functools

import jax
import jax.numpy as jnp
from jax import lax
from jax.experimental import pallas as pl
from jax.experimental.pallas import tpu as pltpu
from jax.sharding import PartitionSpec as P

MESH = pl.DeviceIdType.MESH
F32 = jnp.float32
BF16 = jnp.bfloat16
AXES = ("grp", "ctx")
LOG2E = 1.4426950408889634
BLOCKED = -1e30


def contract(a, b, a_dim, b_dim):
    return lax.dot_general(a, b, (((a_dim,), (b_dim,)), ((), ())), preferred_element_type=F32)


def kernel(
    grps, ctxs, group, scale,
    q_hbm, g_hbm, k_rows, v_rows, ids,
    dq, dk_rows, dv_rows,
    q_all, g_all, rows32, near, ids_in, bias, keep,
    acc_k, acc_v, own_sum, tx, rx,
    q_sem, g_sem, send_near, recv_near, send_ids, recv_ids, send_part, recv_part,
):
    tok = q_all.shape[1]
    kvs = near.shape[1]
    count = grps * ctxs
    me = lax.axis_index("grp") * ctxs + lax.axis_index("ctx")

    def at(offset):
        other = lax.rem(me + (offset + count), count)
        return (other // ctxs, lax.rem(other, ctxs))

    barrier = pltpu.get_barrier_semaphore()
    for offset in (1, -1, 3, -3):
        pl.semaphore_signal(barrier, inc=1, device_id=at(offset), device_id_type=MESH)

    def load(c):
        heads = pl.ds(c * group, group)
        return (
            pltpu.make_async_copy(q_hbm.at[heads], q_all.at[heads], q_sem.at[c]),
            pltpu.make_async_copy(g_hbm.at[heads], g_all.at[heads], g_sem.at[c]),
        )

    for c in range(kvs):
        for copy in load(c):
            copy.start()

    for which, rows in ((0, k_rows), (1, v_rows)):
        rows32[which] = rows[...].astype(F32)
        for c in range(kvs):
            near[0, c, which] = rows32[which, pl.ds(c, tok, stride=kvs), :].astype(BF16)
    ids_in[0] = ids[...]

    pl.semaphore_wait(barrier, 4)

    def remote(src, dst, send, recv, offset):
        return pltpu.make_async_remote_copy(
            src_ref=src, dst_ref=dst, send_sem=send, recv_sem=recv,
            device_id=at(offset), device_id_type=MESH,
        )

    def ids_to(slot, source, offset):
        return remote(ids_in.at[source], ids_in.at[slot], send_ids.at[slot], recv_ids.at[slot], offset)

    def direct(c, slot):
        return remote(near.at[0, c], near.at[slot, c], send_near.at[slot, c], recv_near.at[slot, c], slot)

    def relayed(c, which):
        source, offset = ((1, 1), (3, -1))[which]
        slot = (0, 2)[which]
        return remote(
            near.at[source, c, which], near.at[2, c, which],
            send_near.at[slot, c], recv_near.at[slot, c], offset,
        )

    def part(c, kind):
        offset = (-1, 1, -1, -1, -3, -3)[kind]
        return remote(tx.at[c, kind], rx.at[c, kind], send_part.at[kind, c], recv_part.at[kind, c], offset)

    ids_to(1, 0, 1).start()
    ids_to(3, 0, 3).start()
    for c in range(kvs):
        direct(c, 1).start()
        direct(c, 3).start()
    ids_to(1, 0, 1).wait_recv()
    ids_to(2, 1, 1).start()

    def relay(c):
        direct(c, 1).wait_recv()
        relayed(c, 0).start()
        direct(c, 3).wait_recv()
        relayed(c, 1).start()

    relay(0)

    rows_at = lax.broadcasted_iota(jnp.int32, (tok, tok), 0)
    cols_at = lax.broadcasted_iota(jnp.int32, (tok, tok), 1)
    keep[0] = jnp.where(cols_at <= rows_at, 1.0, 0.0).astype(BF16)
    keep[1] = jnp.where(cols_at <= rows_at, 0.0, 1.0).astype(BF16)
    ids_to(3, 0, 3).wait_recv()
    ids_to(2, 1, 1).wait_recv()
    q_ids = jnp.transpose(jnp.broadcast_to(ids_in[0].astype(F32), (tok, tok)))

    def bias_of(slot):
        return jnp.where(jnp.broadcast_to(ids_in[slot].astype(F32), (tok, tok)) == q_ids, 0.0, BLOCKED)

    bias[0] = jnp.where(cols_at <= rows_at, bias_of(0), bias_of(3))
    bias[1] = bias_of(1)
    bias[2] = bias_of(2)

    def one_head(c, i):
        h = c * group + i
        q = q_all[h]
        g = g_all[h]
        lower = lax.broadcasted_iota(jnp.int32, (tok, tok), 1) <= lax.broadcasted_iota(jnp.int32, (tok, tok), 0)
        s = [contract(q, near[o, c, 0], 1, 1) for o in range(4)]
        s = [jnp.where(lower, s[0], s[3]), s[1], s[2]]
        s = [s[o] * (scale * LOG2E) + bias[o] for o in range(3)]
        peak = jnp.max(jnp.maximum(jnp.maximum(s[0], s[1]), s[2]), axis=1, keepdims=True)
        p = [jnp.exp2(x - peak) for x in s]
        inverse = 1.0 / jnp.sum(p[0] + p[1] + p[2], axis=1, keepdims=True)
        d = [contract(g, near[o, c, 1], 1, 1) for o in range(4)]
        d = [jnp.where(lower, d[0], d[3]), d[1], d[2]]
        p = [x * inverse for x in p]
        center = jnp.sum(p[0] * d[0] + p[1] * d[1] + p[2] * d[2], axis=1, keepdims=True)
        ds = [(p[o] * (d[o] - center)).astype(BF16) for o in range(3)]
        p = [x.astype(BF16) for x in p]
        ds = [ds[0] * keep[0], ds[1], ds[2], ds[0] * keep[1]]
        p = [p[0] * keep[0], p[1], p[2], p[0] * keep[1]]
        total = contract(ds[0], near[0, c, 0], 1, 0)
        for o in range(1, 4):
            total = total + contract(ds[o], near[o, c, 0], 1, 0)
        dq[h] = (total * scale).astype(BF16)
        q_turned = jnp.transpose(q.astype(F32)).astype(BF16)
        g_turned = jnp.transpose(g.astype(F32)).astype(BF16)
        for o in range(4):
            dk = contract(q_turned, ds[o], 1, 0)
            dv = contract(g_turned, p[o], 1, 0)
            if i == 0:
                acc_k[o] = dk
                acc_v[o] = dv
            else:
                acc_k[o] += dk
                acc_v[o] += dv

    def middle(c):
        part(c, 0).wait_recv()
        tx[c, 2] = (own_sum[c, 2] + rx[c, 0].astype(F32)).astype(BF16)
        part(c, 2).start()
        part(c, 1).wait_recv()
        tx[c, 5] = (own_sum[c, 3] + rx[c, 1].astype(F32)).astype(BF16)
        part(c, 5).start()

    def finish(c):
        for kind in (3, 4, 2, 5):
            part(c, kind).wait_recv()
        rows32[0, pl.ds(c, tok, stride=kvs), :] = own_sum[c, 0] + (rx[c, 2].astype(F32) + rx[c, 4].astype(F32))
        rows32[1, pl.ds(c, tok, stride=kvs), :] = own_sum[c, 1] + (rx[c, 3].astype(F32) + rx[c, 5].astype(F32))

    def chunk(c, carry):
        relayed(c, 0).wait_recv()
        relayed(c, 1).wait_recv()
        for copy in load(c):
            copy.wait()
        for i in range(group):
            if i == group // 2:
                pl.when(c < kvs - 1)(lambda: relay(c + 1))
                pl.when(c > 0)(lambda: middle(c - 1))
            one_head(c, i)
        tx[c, 0] = (jnp.transpose(acc_k[2]) * scale).astype(BF16)
        part(c, 0).start()
        tx[c, 1] = jnp.transpose(acc_v[2]).astype(BF16)
        part(c, 1).start()
        tx[c, 3] = jnp.transpose(acc_v[1]).astype(BF16)
        part(c, 3).start()
        tx[c, 4] = (jnp.transpose(acc_k[3]) * scale).astype(BF16)
        part(c, 4).start()
        own_sum[c, 2] = jnp.transpose(acc_k[1]) * scale
        own_sum[c, 3] = jnp.transpose(acc_v[3])
        own_sum[c, 0] = jnp.transpose(acc_k[0]) * scale
        own_sum[c, 1] = jnp.transpose(acc_v[0])
        return carry

    lax.fori_loop(0, kvs, chunk, 0)
    middle(kvs - 1)

    def wrap_up(c, carry):
        finish(c)
        direct(c, 1).wait_send()
        direct(c, 3).wait_send()
        relayed(c, 0).wait_send()
        relayed(c, 1).wait_send()
        for kind in range(6):
            part(c, kind).wait_send()
        return carry

    lax.fori_loop(0, kvs, wrap_up, 0)
    ids_to(1, 0, 1).wait_send()
    ids_to(3, 0, 3).wait_send()
    ids_to(2, 1, 1).wait_send()
    dk_rows[...] = rows32[0].astype(BF16)
    dv_rows[...] = rows32[1].astype(BF16)


def shards(grps, ctxs, queries, key_rows, value_rows, out_grad, doc_ids):
    tok, heads, width = queries.shape
    kvs = key_rows.shape[1]
    vmem = pl.BlockSpec(memory_space=pltpu.VMEM)
    anywhere = pl.BlockSpec(memory_space=pl.ANY)
    dma = pltpu.SemaphoreType.DMA
    dq, dk, dv = pl.pallas_call(
        functools.partial(kernel, grps, ctxs, heads // kvs, width ** -0.5),
        out_shape=(
            jax.ShapeDtypeStruct((heads, tok, width), BF16),
            jax.ShapeDtypeStruct((tok * kvs, width), BF16),
            jax.ShapeDtypeStruct((tok * kvs, width), BF16),
        ),
        in_specs=[anywhere, anywhere, vmem, vmem, vmem],
        out_specs=[vmem, vmem, vmem],
        scratch_shapes=[
            pltpu.VMEM((heads, tok, width), BF16),
            pltpu.VMEM((heads, tok, width), BF16),
            pltpu.VMEM((2, tok * kvs, width), F32),
            pltpu.VMEM((4, kvs, 2, tok, width), BF16),
            pltpu.VMEM((4, 1, tok), jnp.int32),
            pltpu.VMEM((3, tok, tok), F32),
            pltpu.VMEM((2, tok, tok), BF16),
            pltpu.VMEM((4, width, tok), F32),
            pltpu.VMEM((4, width, tok), F32),
            pltpu.VMEM((kvs, 4, tok, width), F32),
            pltpu.VMEM((kvs, 6, tok, width), BF16),
            pltpu.VMEM((kvs, 6, tok, width), BF16),
            dma((kvs,)), dma((kvs,)),
            dma((4, kvs)), dma((4, kvs)),
            dma((4,)), dma((4,)),
            dma((6, kvs)), dma((6, kvs)),
        ],
        compiler_params=pltpu.CompilerParams(
            collective_id=0, has_side_effects=True, vmem_limit_bytes=56 * 2**20
        ),
    )(
        jnp.transpose(queries, (1, 0, 2)),
        jnp.transpose(out_grad, (1, 0, 2)),
        key_rows.reshape(tok * kvs, width),
        value_rows.reshape(tok * kvs, width),
        doc_ids.reshape(1, tok),
    )
    return (
        jnp.transpose(dq, (1, 0, 2)),
        dk.reshape(tok, kvs, width),
        dv.reshape(tok, kvs, width),
    )


def solution(mesh):
    spec = P(AXES, None, None)
    return jax.shard_map(
        functools.partial(shards, mesh.shape["grp"], mesh.shape["ctx"]),
        mesh=mesh,
        in_specs=(spec, spec, spec, spec, P(AXES)),
        out_specs=(spec, spec, spec),
        check_vma=False,
    )
```

profile of v0, /device:TPU:1, one launch (start us, length us, event | category | flops | bytes accessed | tf_op | source)
XLA Modules:
  0.0 84.6 jit_solution(6275467831699600161)
XLA Ops:
  0.6 79.5 %shard_map.76 = (bf16[28,256,128]{2,1,0:T(8,128)(2,1)}, bf16[1024,128]{1,0:T(8,128)(2,1)}, bf16[1024,128]{1,0:T(8,128)(2,1)}) custom-call(bf16[28,256,128]{2,1,0:T(8,128)(2,1)} %bitcast.8, bf16[28,256,128]{2,1,0:T(8,128)(2,1)} %bitcast.9, bf16[1024,128]{1,0:T(8,128)(2,1)} %bitcast.11, bf16[1024,128]{1,0:T(8,128)(2,1)} %bitcast.12, s32[1,256]{1,0:T(1,128)} %bitcast.15), custom_call_target="tpu_custom_call" | custom-call | tf_op jit(solution)/shard_map/pallas_call | solution.py:217
  80.2 0.0 copy-start.1
  80.2 0.0 copy-start
  80.2 3.0 %copy.11 = bf16[256,28,128]{2,0,1:T(8,128)(2,1)} copy(bf16[256,28,128]{2,0,1:T(8,128)(2,1)} %bitcast.10) | data formatting | bytes 3670016
  83.2 0.0 copy-done.1
  83.2 0.7 copy.12
  83.9 0.0 copy-done
  83.9 0.7 copy.13
Async XLA Ops:
  80.2 3.0 %copy-start.1 = (bf16[1024,128]{1,0:T(8,128)(2,1)S(1)}, bf16[1024,128]{1,0:T(8,128)(2,1)}, u32[]{:S(2)}) copy-start(bf16[1024,128]{1,0:T(8,128)(2,1)} %get-tuple-element.7) | copy-start | bytes 786436
  80.2 3.7 %copy-start = (bf16[1024,128]{1,0:T(8,128)(2,1)S(1)}, bf16[1024,128]{1,0:T(8,128)(2,1)}, u32[]{:S(2)}) copy-start(bf16[1024,128]{1,0:T(8,128)(2,1)} %get-tuple-element.8) | copy-start | bytes 786436
where the time goes:
time: 84.7 us; the launch traced here: 84.6 us
  Pallas kernels  79.5 us (94%)
  local copies, waits for them, and re-layouts  4.4 us (5%)
    pallas_call x1, Pallas kernels, shards(): pl.pallas_call(functools.partial(kernel, grps, ctxs, heads // kvs, width...  79.5 us
    unnamed x7, local copies, waits for them, and re-layouts  4.4 us

commit v1 on v0

v1 whole, which is shorter than its diff:
```python
import functools

import jax
import jax.numpy as jnp
from jax import lax
from jax.experimental import pallas as pl
from jax.experimental.pallas import tpu as pltpu
from jax.sharding import PartitionSpec as P

MESH = pl.DeviceIdType.MESH
F32 = jnp.float32
BF16 = jnp.bfloat16
AXES = ("grp", "ctx")
LOG2E = 1.4426950408889634
BLOCKED = -1e30
RING = 4


def contract(a, b, a_dim, b_dim):
    return lax.dot_general(a, b, (((a_dim,), (b_dim,)), ((), ())), preferred_element_type=F32)


def kernel(
    grps, ctxs, group, scale,
    q_hbm, g_hbm, k_rows, v_rows, ids,
    dq, dk_rows, dv_rows,
    q_all, g_all, rows32, near, ids_in, hot, blocked,
    s_a, s_b, d_a, d_b, ds_all, p_all, q_turned, g_turned, inv_all,
    passing, own_sum, tx, rx,
    q_sem, g_sem, send_near, recv_near, send_ids, recv_ids, send_part, recv_part,
):
    tok = q_all.shape[1]
    kvs = near.shape[0]
    half = tok // 2
    width = q_all.shape[2]
    count = grps * ctxs
    me = lax.axis_index("grp") * ctxs + lax.axis_index("ctx")
    place = lax.rem(me, RING)

    def at(offset):
        other = lax.rem(me + (offset + count), count)
        return (other // ctxs, lax.rem(other, ctxs))

    barrier = pltpu.get_barrier_semaphore()
    for offset in (1, -1, 3, -3, RING, -RING):
        pl.semaphore_signal(barrier, inc=1, device_id=at(offset), device_id_type=MESH)

    def load(c):
        heads = pl.ds(c * group, group)
        return (
            pltpu.make_async_copy(q_hbm.at[heads], q_all.at[heads], q_sem.at[c]),
            pltpu.make_async_copy(g_hbm.at[heads], g_all.at[heads], g_sem.at[c]),
        )

    for c in range(kvs):
        for copy in load(c):
            copy.start()

    def block(slot):
        return pl.ds(slot * tok, tok)

    for which, rows in ((0, k_rows), (1, v_rows)):
        rows32[which] = rows[...].astype(F32)
        for c in range(kvs):
            near[c, which, block(0)] = rows32[which, pl.ds(c, tok, stride=kvs), :].astype(BF16)
    ids_in[0] = ids[...]

    pl.semaphore_wait(barrier, 6)

    def remote(src, dst, send, recv, offset):
        return pltpu.make_async_remote_copy(
            src_ref=src, dst_ref=dst, send_sem=send, recv_sem=recv,
            device_id=at(offset), device_id_type=MESH,
        )

    def ids_to(slot, source, offset):
        return remote(ids_in.at[source], ids_in.at[slot], send_ids.at[slot], recv_ids.at[slot], offset)

    moves = ((0, 0, 1, 1), (0, 0, 3, 3), (1, 0, 3, 3), (1, 0, 1, 1), (0, 1, 2, 1), (1, 3, 2, -1))

    def move(c, kind):
        which, source, slot, offset = moves[kind]
        return remote(
            near.at[c, which, block(source)], near.at[c, which, block(slot)],
            send_near.at[kind, c], recv_near.at[kind, c], offset,
        )

    def onward(c, which):
        return remote(
            near.at[c, which, block(0)], passing.at[c, which],
            send_near.at[6 + which, c], recv_near.at[6 + which, c], RING,
        )

    def handed(c, kind):
        which, _, slot, offset = moves[kind]
        return remote(
            passing.at[c, which], near.at[c, which, block(slot)],
            send_near.at[kind, c], recv_near.at[kind, c], offset - RING,
        )

    def feed(c):
        @pl.when(place == RING - 1)
        def _():
            for which in range(2):
                onward(c, which).start()

        @pl.when(place != RING - 1)
        def _():
            for kind in range(4):
                move(c, kind).start()

    def forward(c):
        @pl.when(place == RING - 1)
        def _():
            onward(c, 0).wait_recv()
            handed(c, 0).start()
            handed(c, 1).start()
            onward(c, 1).wait_recv()
            handed(c, 2).start()
            handed(c, 3).start()

    def relay(c):
        move(c, 0).wait_recv()
        move(c, 4).start()
        move(c, 2).wait_recv()
        move(c, 5).start()

    def part(c, kind, shift=0):
        offset = (-1, 1, -1, -1, -3, -3, -RING, -RING)[kind] + shift
        return remote(tx.at[c, kind], rx.at[c, kind], send_part.at[kind, c], recv_part.at[kind, c], offset)

    def give(c, kind):
        turn = (0, 0, 0, 0, 2, 2)[kind]

        @pl.when(place == turn)
        def _():
            part(c, kind, RING).start()

        @pl.when(place != turn)
        def _():
            part(c, kind).start()

    def join(c):
        @pl.when(place == RING - 1)
        def _():
            for kind in (2, 4):
                part(c, kind).wait_recv()
            tx[c, 6] = (rx[c, 2].astype(F32) + rx[c, 4].astype(F32)).astype(BF16)
            part(c, 6).start()
            for kind in (3, 5):
                part(c, kind).wait_recv()
            tx[c, 7] = (rx[c, 3].astype(F32) + rx[c, 5].astype(F32)).astype(BF16)
            part(c, 7).start()

    ids_to(1, 0, 1).start()
    ids_to(3, 0, 3).start()
    feed(0)
    ids_to(1, 0, 1).wait_recv()
    ids_to(2, 1, 1).start()
    forward(0)
    feed(1)
    relay(0)
    forward(1)
    feed(2)

    lanes = lax.broadcasted_iota(jnp.int32, (tok, width), 1).astype(F32)

    def column(slot):
        return jnp.transpose(jnp.broadcast_to(ids_in[slot].astype(F32), (width, tok)))

    hot[...] = jnp.where(column(0) == lanes, 1.0, 0.0).astype(BF16)
    ids_to(3, 0, 3).wait_recv()
    ids_to(2, 1, 1).wait_recv()
    for slot in range(4):
        blocked[block(slot)] = jnp.where(column(slot) == lanes, 0.0, BLOCKED).astype(BF16)
    low = lax.broadcasted_iota(jnp.int32, (half, half), 1) <= lax.broadcasted_iota(jnp.int32, (half, half), 0)
    keep = [jnp.where(low, 1.0, 0.0).astype(BF16), jnp.where(low, 0.0, 1.0).astype(BF16)]

    def corners(ref):
        for i in range(group):
            ref[i * tok:i * tok + half, half:tok] = jnp.zeros((half, half), BF16)
            ref[i * tok + half:(i + 1) * tok, 3 * tok:3 * tok + half] = jnp.zeros((half, half), BF16)

    corners(p_all)
    for c in range(kvs):
        corners(ds_all.at[c])

    def products(c, h, slot, step):
        q = jnp.concatenate([q_all[h], hot[...]], axis=1)
        g = g_all[h]
        for out, rows, right in (
            ((s_a, s_b)[slot], q, lambda o: jnp.concatenate([near[c, 0, block(o)], blocked[block(o)]], axis=1)),
            ((d_a, d_b)[slot], g, lambda o: near[c, 1, block(o)]),
        ):
            if step in (1, 2):
                out[:, step * tok:(step + 1) * tok] = contract(rows, right(step), 1, 1)
            if step == 0:
                own = contract(rows, right(0), 1, 1)
                third = contract(rows, right(3), 1, 1)
                out[:half, :half] = jnp.where(low, own[:half, :half], third[:half, :half])
                out[:half, half:tok] = third[:half, half:]
                out[half:, :half] = own[half:, :half]
                out[half:, half:tok] = jnp.where(low, own[half:, half:], third[half:, half:])

    steps = 8
    some = tok // steps

    def spread(ref, i, first, x):
        rows = slice(i * tok + first, i * tok + first + some)
        part_of = slice(first % half, first % half + some)
        ref[rows, tok:3 * tok] = x[:, tok:]
        if first < half:
            ref[rows, :half] = x[:, :half] * keep[0][part_of]
            ref[rows, 3 * tok:3 * tok + half] = x[:, :half] * keep[1][part_of]
            ref[rows, 3 * tok + half:] = x[:, half:tok]
        else:
            ref[rows, :half] = x[:, :half]
            ref[rows, half:tok] = x[:, half:tok] * keep[0][part_of]
            ref[rows, 3 * tok + half:] = x[:, half:tok] * keep[1][part_of]

    def softmax(c, h, i, step):
        first = step * some
        rows = slice(first, first + some)
        s = (s_a, s_b)[i % 2][rows]
        d = (d_a, d_b)[i % 2][rows]
        peak = jnp.max(s, axis=1, keepdims=True)
        p = jnp.exp2((s - peak) * (scale * LOG2E))
        inverse = 1.0 / jnp.sum(p, axis=1, keepdims=True)
        center = jnp.sum(p * d, axis=1, keepdims=True) * inverse
        spread(ds_all.at[c], i, first, (p * (d - center)).astype(BF16))
        spread(p_all, i, first, p.astype(BF16))
        inv_all[c, i * tok + first:i * tok + first + some] = jnp.broadcast_to(inverse, (some, width))
        if step == steps - 1:
            head = slice(i * tok, (i + 1) * tok)
            q_turned[:, head] = jnp.transpose(q_all[h].astype(F32) * inv_all[c, head]).astype(BF16)
            g_turned[:, head] = jnp.transpose(g_all[h].astype(F32) * inv_all[c, head]).astype(BF16)

    def query_part(c, h, i):
        head = slice(i * tok, (i + 1) * tok)
        dq[h] = (contract(ds_all[c, head], near[c, 0], 1, 0) * (inv_all[c, head] * scale)).astype(BF16)

    def key_part(c, slot):
        x = contract(q_turned[...], ds_all[c, :, slot * tok:(slot + 1) * tok], 1, 0)
        return jnp.transpose(x) * scale

    def value_part(slot):
        x = contract(g_turned[...], p_all[:, slot * tok:(slot + 1) * tok], 1, 0)
        return jnp.transpose(x)

    def interleave(*items):
        for step in range(steps):
            for work, args, number in items:
                for one in range(step * number // steps, (step + 1) * number // steps):
                    work(*args, one)

    def middle(c):
        part(c, 0).wait_recv()
        tx[c, 2] = (own_sum[c, 2] + rx[c, 0].astype(F32)).astype(BF16)
        give(c, 2)
        part(c, 1).wait_recv()
        tx[c, 5] = (own_sum[c, 3] + rx[c, 1].astype(F32)).astype(BF16)
        give(c, 5)

    def finish(c):
        def total(which, kinds):
            for kind in kinds:
                part(c, kind).wait_recv()
            x = rx[c, kinds[0]].astype(F32)
            for kind in kinds[1:]:
                x = x + rx[c, kind].astype(F32)
            rows32[which, pl.ds(c, tok, stride=kvs), :] = own_sum[c, which] + x

        @pl.when(place == RING - 1)
        def _():
            total(0, (6,))
            total(1, (7,))

        @pl.when(place != RING - 1)
        def _():
            total(0, (2, 4))
            total(1, (3, 5))

    def chunk(c, carry):
        for kind in (1, 3, 4, 5):
            move(c, kind).wait_recv()
        for copy in load(c):
            copy.wait()

        def first(i):
            return (products, (c, c * group + i, i % 2), 4)

        def second(i):
            return (softmax, (c, c * group + i, i), steps)

        events = ((3, 1, relay), (5, 2, forward), (5, 3, feed), (4, -2, join), (6, -1, middle))
        interleave(first(0))
        interleave(second(0), first(1))
        for i in range(2, group):
            for when, ahead, event in events:
                if when == i:
                    pl.when((c + ahead >= 0) & (c + ahead < kvs))(functools.partial(event, c + ahead))
            interleave(second(i - 1), first(i))
        interleave(second(group - 1))
        tx[c, 0] = key_part(c, 2).astype(BF16)
        part(c, 0).start()
        tx[c, 1] = value_part(2).astype(BF16)
        part(c, 1).start()
        tx[c, 3] = value_part(1).astype(BF16)
        give(c, 3)
        tx[c, 4] = key_part(c, 3).astype(BF16)
        give(c, 4)
        own_sum[c, 2] = key_part(c, 1)
        own_sum[c, 3] = value_part(3)
        own_sum[c, 0] = key_part(c, 0)
        own_sum[c, 1] = value_part(0)
        return carry

    def queries_of(c, carry):
        for i in range(group):
            query_part(c, c * group + i, i)
        return carry

    lax.fori_loop(0, kvs, chunk, 0)
    lax.fori_loop(0, kvs // 2, queries_of, 0)
    join(kvs - 2)
    middle(kvs - 1)
    join(kvs - 1)
    lax.fori_loop(kvs // 2, kvs, queries_of, 0)

    def wrap_up(c, carry):
        finish(c)
        for kind in range(6):
            move(c, kind).wait_send()
            part(c, kind).wait_send()

        @pl.when(place == RING - 1)
        def _():
            for which in range(2):
                onward(c, which).wait_send()
                part(c, 6 + which).wait_send()

        return carry

    lax.fori_loop(0, kvs, wrap_up, 0)
    ids_to(1, 0, 1).wait_send()
    ids_to(3, 0, 3).wait_send()
    ids_to(2, 1, 1).wait_send()
    dk_rows[...] = rows32[0].astype(BF16)
    dv_rows[...] = rows32[1].astype(BF16)


def shards(grps, ctxs, queries, key_rows, value_rows, out_grad, doc_ids):
    tok, heads, width = queries.shape
    kvs = key_rows.shape[1]
    group = heads // kvs
    vmem = pl.BlockSpec(memory_space=pltpu.VMEM)
    anywhere = pl.BlockSpec(memory_space=pl.ANY)
    dma = pltpu.SemaphoreType.DMA
    dq, dk, dv = pl.pallas_call(
        functools.partial(kernel, grps, ctxs, group, width ** -0.5),
        out_shape=(
            pltpu.VMEM((heads, tok, width), BF16),
            jax.ShapeDtypeStruct((tok * kvs, width), BF16),
            jax.ShapeDtypeStruct((tok * kvs, width), BF16),
        ),
        in_specs=[anywhere, anywhere, vmem, vmem, vmem],
        out_specs=[vmem, vmem, vmem],
        scratch_shapes=[
            pltpu.VMEM((heads, tok, width), BF16),
            pltpu.VMEM((heads, tok, width), BF16),
            pltpu.VMEM((2, tok * kvs, width), F32),
            pltpu.VMEM((kvs, 2, 4 * tok, width), BF16),
            pltpu.VMEM((4, 1, tok), jnp.int32),
            pltpu.VMEM((tok, width), BF16),
            pltpu.VMEM((4 * tok, width), BF16),
            pltpu.VMEM((tok, 3 * tok), F32),
            pltpu.VMEM((tok, 3 * tok), F32),
            pltpu.VMEM((tok, 3 * tok), F32),
            pltpu.VMEM((tok, 3 * tok), F32),
            pltpu.VMEM((kvs, group * tok, 4 * tok), BF16),
            pltpu.VMEM((group * tok, 4 * tok), BF16),
            pltpu.VMEM((width, group * tok), BF16),
            pltpu.VMEM((width, group * tok), BF16),
            pltpu.VMEM((kvs, group * tok, width), F32),
            pltpu.VMEM((kvs, 2, tok, width), BF16),
            pltpu.VMEM((kvs, 4, tok, width), F32),
            pltpu.VMEM((kvs, 8, tok, width), BF16),
            pltpu.VMEM((kvs, 8, tok, width), BF16),
            dma((kvs,)), dma((kvs,)),
            dma((8, kvs)), dma((8, kvs)),
            dma((4,)), dma((4,)),
            dma((8, kvs)), dma((8, kvs)),
        ],
        compiler_params=pltpu.CompilerParams(
            collective_id=0, has_side_effects=True, vmem_limit_bytes=56 * 2**20
        ),
    )(
        jnp.transpose(queries, (1, 0, 2)),
        jnp.transpose(out_grad, (1, 0, 2)),
        key_rows.reshape(tok * kvs, width),
        value_rows.reshape(tok * kvs, width),
        doc_ids.reshape(1, tok),
    )
    return (
        jnp.transpose(dq, (1, 0, 2)),
        dk.reshape(tok, kvs, width),
        dv.reshape(tok, kvs, width),
    )


def solution(mesh):
    spec = P(AXES, None, None)
    return jax.shard_map(
        functools.partial(shards, mesh.shape["grp"], mesh.shape["ctx"]),
        mesh=mesh,
        in_specs=(spec, spec, spec, spec, P(AXES)),
        out_specs=(spec, spec, spec),
        check_vma=False,
    )
```

time: 84.7 us -> 65 us (0.77)
  the two profiles are of different devices: /device:TPU:1 before, /device:TPU:24 now
where the time goes in v1:
time: 65 us; the launch traced here: 64.9 us
  Pallas kernels  61.6 us (95%)
  local copies, waits for them, and re-layouts  2.64 us (4%)
  between operations  0.66 us (1%)
    pallas_call x1, Pallas kernels, shards(): pl.pallas_call(functools.partial(kernel, grps, ctxs, group, width ** (-0....  61.6 us
    unnamed x7, local copies, waits for them, and re-layouts  2.64 us

profile of v1, /device:TPU:24, one launch (start us, length us, event | category | flops | bytes accessed | tf_op | source)
XLA Modules:
  0.0 64.9 jit_solution(13257579061652297180)
XLA Ops:
  0.6 61.6 %shard_map.76 = (bf16[28,256,128]{2,1,0:T(8,128)(2,1)S(1)}, bf16[1024,128]{1,0:T(8,128)(2,1)}, bf16[1024,128]{1,0:T(8,128)(2,1)}) custom-call(bf16[28,256,128]{2,1,0:T(8,128)(2,1)} %bitcast.9, bf16[28,256,128]{2,1,0:T(8,128)(2,1)} %bitcast.10, bf16[1024,128]{1,0:T(8,128)(2,1)} %bitcast.11, bf16[1024,128]{1,0:T(8,128)(2,1)} %bitcast.12, s32[1,256]{1,0:T(1,128)} %bitcast.15), custom_call_target="tpu_custom_call" | custom-call | tf_op jit(solution)/shard_map/pallas_call | solution.py:359
  62.3 0.0 copy-start.1
  62.3 0.0 copy-start
  62.3 1.2 %copy.11 = bf16[256,28,128]{2,0,1:T(8,128)(2,1)} copy(bf16[256,28,128]{2,0,1:T(8,128)(2,1)S(1)} %bitcast.8) | data formatting | bytes 3670016
  63.5 0.0 copy-done.1
  63.5 0.7 %copy.12 = bf16[256,4,128]{2,1,0:T(4,128)(2,1)} copy(bf16[256,4,128]{2,1,0:T(4,128)(2,1)S(1)} %bitcast.14) | data formatting | bytes 524288
  64.2 0.0 copy-done
  64.2 0.7 %copy.13 = bf16[256,4,128]{2,1,0:T(4,128)(2,1)} copy(bf16[256,4,128]{2,1,0:T(4,128)(2,1)S(1)} %bitcast.13) | data formatting | bytes 524288
Async XLA Ops:
  62.3 1.3 %copy-start.1 = (bf16[1024,128]{1,0:T(8,128)(2,1)S(1)}, bf16[1024,128]{1,0:T(8,128)(2,1)}, u32[]{:S(2)}) copy-start(bf16[1024,128]{1,0:T(8,128)(2,1)} %get-tuple-element.7) | copy-start | bytes 786436
  62.3 1.9 %copy-start = (bf16[1024,128]{1,0:T(8,128)(2,1)S(1)}, bf16[1024,128]{1,0:T(8,128)(2,1)}, u32[]{:S(2)}) copy-start(bf16[1024,128]{1,0:T(8,128)(2,1)} %get-tuple-element.8) | copy-start | bytes 786436

commit v2 on v1

--- a/solution.py
+++ b/solution.py
@@ -22,12 +22,12 @@
 
 def kernel(
     grps, ctxs, group, scale,
-    q_hbm, g_hbm, k_rows, v_rows, ids,
+    q_hbm, g_hbm, k_hbm, v_hbm, ids,
     dq, dk_rows, dv_rows,
-    q_all, g_all, rows32, near, ids_in, hot, blocked,
+    q_all, g_all, k_rows, v_rows, rows32, near, ids_in, hot, blocked,
     s_a, s_b, d_a, d_b, ds_all, p_all, q_turned, g_turned, inv_all,
     passing, own_sum, tx, rx,
-    q_sem, g_sem, send_near, recv_near, send_ids, recv_ids, send_part, recv_part,
+    q_sem, g_sem, rows_sem, send_near, recv_near, send_ids, recv_ids, send_part, recv_part,
 ):
     tok = q_all.shape[1]
     kvs = near.shape[0]
@@ -52,6 +52,12 @@
             pltpu.make_async_copy(g_hbm.at[heads], g_all.at[heads], g_sem.at[c]),
         )
 
+    rows_in = [
+        pltpu.make_async_copy(hbm, rows, rows_sem.at[which])
+        for which, (hbm, rows) in enumerate(((k_hbm, k_rows), (v_hbm, v_rows)))
+    ]
+    for copy in rows_in:
+        copy.start()
     for c in range(kvs):
         for copy in load(c):
             copy.start()
@@ -59,10 +65,14 @@
     def block(slot):
         return pl.ds(slot * tok, tok)
 
+    def split(c):
+        for which in range(2):
+            near[c, which, block(0)] = rows32[which, pl.ds(c, tok, stride=kvs), :].astype(BF16)
+
     for which, rows in ((0, k_rows), (1, v_rows)):
+        rows_in[which].wait()
         rows32[which] = rows[...].astype(F32)
-        for c in range(kvs):
-            near[c, which, block(0)] = rows32[which, pl.ds(c, tok, stride=kvs), :].astype(BF16)
+    split(0)
     ids_in[0] = ids[...]
 
     pl.semaphore_wait(barrier, 6)
@@ -155,6 +165,8 @@
     ids_to(1, 0, 1).start()
     ids_to(3, 0, 3).start()
     feed(0)
+    for c in range(1, kvs):
+        split(c)
     ids_to(1, 0, 1).wait_recv()
     ids_to(2, 1, 1).start()
     forward(0)
@@ -292,7 +304,7 @@
         def second(i):
             return (softmax, (c, c * group + i, i), steps)
 
-        events = ((3, 1, relay), (5, 2, forward), (5, 3, feed), (4, -2, join), (6, -1, middle))
+        events = ((3, 1, relay), (5, 2, forward), (5, 3, feed), (6, -1, middle), (6, -2, join))
         interleave(first(0))
         interleave(second(0), first(1))
         for i in range(2, group):
@@ -320,15 +332,20 @@
             query_part(c, c * group + i, i)
         return carry
 
+    def ended(c, carry):
+        finish(c)
+        return carry
+
     lax.fori_loop(0, kvs, chunk, 0)
-    lax.fori_loop(0, kvs // 2, queries_of, 0)
     join(kvs - 2)
+    lax.fori_loop(0, kvs // 4, queries_of, 0)
     middle(kvs - 1)
+    lax.fori_loop(kvs // 4, kvs, queries_of, 0)
+    lax.fori_loop(0, kvs - 1, ended, 0)
     join(kvs - 1)
-    lax.fori_loop(kvs // 2, kvs, queries_of, 0)
+    finish(kvs - 1)
 
     def wrap_up(c, carry):
-        finish(c)
         for kind in range(6):
             move(c, kind).wait_send()
             part(c, kind).wait_send()
@@ -360,14 +377,16 @@
         functools.partial(kernel, grps, ctxs, group, width ** -0.5),
         out_shape=(
             pltpu.VMEM((heads, tok, width), BF16),
-            jax.ShapeDtypeStruct((tok * kvs, width), BF16),
-            jax.ShapeDtypeStruct((tok * kvs, width), BF16),
+            pltpu.VMEM((tok * kvs, width), BF16),
+            pltpu.VMEM((tok * kvs, width), BF16),
         ),
-        in_specs=[anywhere, anywhere, vmem, vmem, vmem],
+        in_specs=[anywhere, anywhere, anywhere, anywhere, vmem],
         out_specs=[vmem, vmem, vmem],
         scratch_shapes=[
             pltpu.VMEM((heads, tok, width), BF16),
             pltpu.VMEM((heads, tok, width), BF16),
+            pltpu.VMEM((tok * kvs, width), BF16),
+            pltpu.VMEM((tok * kvs, width), BF16),
             pltpu.VMEM((2, tok * kvs, width), F32),
             pltpu.VMEM((kvs, 2, 4 * tok, width), BF16),
             pltpu.VMEM((4, 1, tok), jnp.int32),
@@ -386,7 +405,7 @@
             pltpu.VMEM((kvs, 4, tok, width), F32),
             pltpu.VMEM((kvs, 8, tok, width), BF16),
             pltpu.VMEM((kvs, 8, tok, width), BF16),
-            dma((kvs,)), dma((kvs,)),
+            dma((kvs,)), dma((kvs,)), dma((2,)),
             dma((8, kvs)), dma((8, kvs)),
             dma((4,)), dma((4,)),
             dma((8, kvs)), dma((8, kvs)),

time: 65 us -> 63.9 us (0.983)
  Pallas kernels: 61.6 us -> 60.5 us
    pallas_call x1, Pallas kernels: 61.6 us -> 60.5 us  [shards(): pl.pallas_call(functools.partial(kernel, grps, ctxs, group, width ** (-0....]
    unnamed x7 -> x3, local copies, waits for them, and re-layouts: 2.64 us -> 2.64 us
where the time goes in v2:
time: 63.9 us; the launch traced here: 63.8 us
  Pallas kernels  60.5 us (95%)
  local copies, waits for them, and re-layouts  2.64 us (4%)
  between operations  0.64 us (1%)
    pallas_call x1, Pallas kernels, shards(): pl.pallas_call(functools.partial(kernel, grps, ctxs, group, width ** (-0....  60.5 us
    unnamed x3, local copies, waits for them, and re-layouts  2.64 us

profile of v2, /device:TPU:24, one launch (start us, length us, event | category | flops | bytes accessed | tf_op | source)
XLA Modules:
  0.0 63.8 jit_solution(4443235938206243327)
XLA Ops:
  0.6 60.5 %shard_map.76 = (bf16[28,256,128]{2,1,0:T(8,128)(2,1)S(1)}, bf16[1024,128]{1,0:T(8,128)(2,1)S(1)}, bf16[1024,128]{1,0:T(8,128)(2,1)S(1)}) custom-call(bf16[28,256,128]{2,1,0:T(8,128)(2,1)} %bitcast.11, bf16[28,256,128]{2,1,0:T(8,128)(2,1)} %bitcast.12, bf16[1024,128]{1,0:T(8,128)(2,1)} %bitcast.13, bf16[1024,128]{1,0:T(8,128)(2,1)} %bitcast.14, ...), custom_call_target="tpu_custom_call" | custom-call | tf_op jit(solution)/shard_map/pallas_call | solution.py:376
  61.1 1.2 %copy.11 = bf16[256,28,128]{2,0,1:T(8,128)(2,1)} copy(bf16[256,28,128]{2,0,1:T(8,128)(2,1)S(1)} %bitcast.8) | data formatting | bytes 3670016
  62.4 0.7 %copy.12 = bf16[256,4,128]{2,1,0:T(4,128)(2,1)} copy(bf16[256,4,128]{2,1,0:T(4,128)(2,1)S(1)} %bitcast.10) | data formatting | bytes 524288
  63.1 0.7 %copy.13 = bf16[256,4,128]{2,1,0:T(4,128)(2,1)} copy(bf16[256,4,128]{2,1,0:T(4,128)(2,1)S(1)} %bitcast.9) | data formatting | bytes 524288

commit v3 on v2

--- a/solution.py
+++ b/solution.py
@@ -337,8 +337,8 @@
         return carry
 
     lax.fori_loop(0, kvs, chunk, 0)
+    lax.fori_loop(0, kvs // 4, queries_of, 0)
     join(kvs - 2)
-    lax.fori_loop(0, kvs // 4, queries_of, 0)
     middle(kvs - 1)
     lax.fori_loop(kvs // 4, kvs, queries_of, 0)
     lax.fori_loop(0, kvs - 1, ended, 0)

time: 63.9 us -> 63.8 us (level)
  no operation moved by 1% of the time
where the time goes in v3:
time: 63.8 us; the launch traced here: 63.7 us
  Pallas kernels  60.5 us (95%)
  local copies, waits for them, and re-layouts  2.64 us (4%)
  between operations  0.64 us (1%)
    pallas_call x1, Pallas kernels, shards(): pl.pallas_call(functools.partial(kernel, grps, ctxs, group, width ** (-0....  60.5 us
    unnamed x3, local copies, waits for them, and re-layouts  2.64 us

profile of v3, /device:TPU:24, one launch (start us, length us, event | category | flops | bytes accessed | tf_op | source)
XLA Modules:
  0.0 63.7 jit_solution(7327748049434845115)
XLA Ops:
  0.6 60.5 %shard_map.76 = (bf16[28,256,128]{2,1,0:T(8,128)(2,1)S(1)}, bf16[1024,128]{1,0:T(8,128)(2,1)S(1)}, bf16[1024,128]{1,0:T(8,128)(2,1)S(1)}) custom-call(bf16[28,256,128]{2,1,0:T(8,128)(2,1)} %bitcast.11, bf16[28,256,128]{2,1,0:T(8,128)(2,1)} %bitcast.12, bf16[1024,128]{1,0:T(8,128)(2,1)} %bitcast.13, bf16[1024,128]{1,0:T(8,128)(2,1)} %bitcast.14, ...), custom_call_target="tpu_custom_call" | custom-call | tf_op jit(solution)/shard_map/pallas_call | solution.py:376
  61.1 1.2 %copy.11 = bf16[256,28,128]{2,0,1:T(8,128)(2,1)} copy(bf16[256,28,128]{2,0,1:T(8,128)(2,1)S(1)} %bitcast.8) | data formatting | bytes 3670016
  62.3 0.7 %copy.12 = bf16[256,4,128]{2,1,0:T(4,128)(2,1)} copy(bf16[256,4,128]{2,1,0:T(4,128)(2,1)S(1)} %bitcast.10) | data formatting | bytes 524288
  63.0 0.7 %copy.13 = bf16[256,4,128]{2,1,0:T(4,128)(2,1)} copy(bf16[256,4,128]{2,1,0:T(4,128)(2,1)S(1)} %bitcast.9) | data formatting | bytes 524288
